TPU v7x, 32 devices: a whole 2x2x4 slice. The times are simulated.
32 devices in a mesh: groups: 2 (over y), space: 4 (over z), tangent: 4 (over x, core).
Axes of the slice: x: 2, y: 2, z: 4, core: 2. Of those that a mesh axis runs over, the one named last changes fastest.
Arguments:
- positions: float32 [16, 2, 128], P(('groups', 'space')), parts along dimension 0, may hold values from 0.45 to 15.55, as said below
- momenta: float32 [16, 2, 128], P(('groups', 'space')), parts along dimension 0, may hold values from -4 to 4
- cell_count: int32 [16], P(('groups', 'space')), parts along dimension 0, may hold values from 64 to 128, as said below
- tangent: float32 [16, 4, 128, 1024], P(('groups', 'space'), None, None, 'tangent'), parts along dimension 0, may hold values from -6 to 6
Outputs:
- phase: float32 [16, 4, 128], P(('groups', 'space')), parts along dimension 0
- new_tangent: float32 [16, 4, 128, 1024], P(('groups', 'space'), None, None, 'tangent'), parts along dimension 0
- stretch: float32 [2048], P(('groups', 'tangent')), parts along dimension 0
There are 2 independent parts, one for each index of `groups`. A program takes and returns all parts, laid end to end along the dimension named above; each array names one. Nothing has to cross between parts.
Inputs may be any that keep to these rules, and one draw needn't show every extreme that they name: Slots 0 to cell_count - 1 of a cell hold particles, the others are padding; some cell holds 128 particles in every draw. `positions`: every slot of a cell, padding too, lies within 0.05 in each coordinate of its own point of the lattice (m + 0.5, n + 0.5), m from 0 to 7, n from 0 to 15; no two slots of a cell share a lattice point.
All inputs are finite; a program needn't handle non-finite values.
Results may differ from a plain program's by a relative error of at most 0.006.
Values may be sent and summed in bfloat16 or wider, within the bound.
No kernel may reach another device: no remote copies, remote signals or barrier semaphores. Data moves between devices by JAX's collectives and lax.ppermute only.
A program may use at most 128 MiB of HBM per device.

v0:
```python
import jax
import jax.numpy as jnp
from jax import lax
from jax.sharding import PartitionSpec as P

STEPS = 2
DT = 0.005
CUT2 = 2.0 ** (1.0 / 3.0)
PARK = 1000.0
HIGH = lax.Precision.HIGHEST


def padded(block, sides, width):
    for axis, dim in sides:
        count = lax.axis_size(axis)
        forward = [(i, i + 1) for i in range(count - 1)]
        forward.append((count - 1, 0))
        backward = [(target, source) for source, target in forward]
        low = lax.ppermute(
            lax.slice_in_dim(block, block.shape[dim] - width, None, axis=dim), axis, forward
        )
        high = lax.ppermute(lax.slice_in_dim(block, 0, width, axis=dim), axis, backward)
        block = jnp.concatenate([low, block, high], axis=dim)
    return block


def pair_terms(own_coords, own_alive, far_coords, shift_x, shift_y, same_cell):
    delta_x = shift_x + far_coords[:, 0, None, :] - own_coords[:, 0, :, None]
    delta_y = shift_y + far_coords[:, 1, None, :] - own_coords[:, 1, :, None]
    dist2 = delta_x * delta_x + delta_y * delta_y
    within = jnp.logical_and(dist2 < CUT2, own_alive[:, :, None] > 0.5)
    if same_cell:
        within = jnp.logical_and(within, jnp.logical_not(jnp.eye(dist2.shape[-1], dtype=bool)))
    weight = within.astype(jnp.float32)
    safe = jnp.where(within, dist2, CUT2)
    inverse = 1.0 / safe
    inv_three = inverse * inverse * inverse
    inv_six = inv_three * inv_three
    energy = 4.0 * (inv_six - inv_three) + 1.0
    energy_1 = 4.0 * (3.0 * inv_three - 6.0 * inv_six) * inverse
    energy_2 = 4.0 * (42.0 * inv_six - 12.0 * inv_three) * inverse * inverse
    taper = 1.0 - safe / CUT2
    switch = taper * taper
    switch_1 = -2.0 * taper / CUT2
    switch_2 = 2.0 / (CUT2 * CUT2)
    grad_1 = (energy_1 * switch + energy * switch_1) * weight
    grad_2 = (energy_2 * switch + 2.0 * energy_1 * switch_1 + energy * switch_2) * weight
    pull_x = 2.0 * grad_1 * delta_x
    pull_y = 2.0 * grad_1 * delta_y
    k_xx = (2.0 * grad_1 + 4.0 * grad_2 * delta_x * delta_x).astype(jnp.bfloat16)
    k_xy = (4.0 * grad_2 * delta_x * delta_y).astype(jnp.bfloat16)
    k_yy = (2.0 * grad_1 + 4.0 * grad_2 * delta_y * delta_y).astype(jnp.bfloat16)
    return (pull_x, pull_y, k_xx, k_xy, k_yy)


def apply_rows(k_xx, k_xy, k_yy, far_low):
    gain_x = jnp.einsum(
        "cij,cjv->civ", k_xx, far_low[:, 0], preferred_element_type=jnp.float32
    ) + jnp.einsum("cij,cjv->civ", k_xy, far_low[:, 1], preferred_element_type=jnp.float32)
    gain_y = jnp.einsum(
        "cij,cjv->civ", k_xy, far_low[:, 0], preferred_element_type=jnp.float32
    ) + jnp.einsum("cij,cjv->civ", k_yy, far_low[:, 1], preferred_element_type=jnp.float32)
    return (gain_x, gain_y)


def add_pair(totals, parked, occupied, far_coords, far_low, shift_x, shift_y, same_cell):
    forces_x, forces_y, push_x, push_y, diag_xx, diag_xy, diag_yy = totals
    pull_x, pull_y, k_xx, k_xy, k_yy = pair_terms(
        parked, occupied, far_coords, shift_x, shift_y, same_cell
    )
    gain_x, gain_y = apply_rows(k_xx, k_xy, k_yy, far_low)
    totals = (
        forces_x + jnp.sum(pull_x, axis=2),
        forces_y + jnp.sum(pull_y, axis=2),
        push_x + gain_x,
        push_y + gain_y,
        diag_xx + jnp.sum(k_xx.astype(jnp.float32), axis=2),
        diag_xy + jnp.sum(k_xy.astype(jnp.float32), axis=2),
        diag_yy + jnp.sum(k_yy.astype(jnp.float32), axis=2),
    )
    return (totals, (pull_x, pull_y, k_xx, k_xy, k_yy))


def evaluate(coords, occupied, small_q):
    cell_total = coords.shape[0]
    low = small_q.astype(jnp.bfloat16)
    parked = jnp.concatenate(
        [coords[:, 0:1] + PARK * (1.0 - occupied)[:, None, :], coords[:, 1:2]], axis=1
    )
    empty_rows = jnp.zeros(occupied.shape, jnp.float32)
    empty_push = jnp.zeros(small_q[:, 0].shape, jnp.float32)
    totals = (empty_rows, empty_rows, empty_push, empty_push, empty_rows, empty_rows, empty_rows)
    far_low = padded(low, (("space", 0),), cell_total)
    far_coords = padded(parked, (("space", 0),), cell_total)
    for side in (-1, 0, 1):
        if side == 0:
            block_low = low
            block_coords = parked
        else:
            begin = (1 + side) * cell_total
            block_low = far_low[begin : begin + cell_total]
            block_coords = far_coords[begin : begin + cell_total]
        for lane in (-1, 0, 1):
            totals, unused = add_pair(
                totals,
                parked,
                occupied,
                jnp.roll(block_coords, -lane, axis=0),
                jnp.roll(block_low, -lane, axis=0),
                8.0 * side,
                16.0 * lane,
                side == 0 and lane == 0,
            )
    forces_x, forces_y, push_x, push_y, diag_xx, diag_xy, diag_yy = totals
    wide_own = low.astype(jnp.float32)
    push_x = push_x - diag_xx[..., None] * wide_own[:, 0] - diag_xy[..., None] * wide_own[:, 1]
    push_y = push_y - diag_xy[..., None] * wide_own[:, 0] - diag_yy[..., None] * wide_own[:, 1]
    forces = jnp.stack([forces_x, forces_y], axis=1)
    pushes = jnp.stack([push_x, push_y], axis=1)
    return (forces, pushes)


def body(positions, momenta, cell_count, tangent):
    cell_total = positions.shape[0]
    slot_count = positions.shape[2]
    block_cols = tangent.shape[3]
    occupied = (
        lax.broadcasted_iota(jnp.int32, (cell_total, slot_count), 1) < cell_count[:, None]
    ).astype(jnp.float32)
    state = tangent * occupied[:, None, :, None]
    coords = positions
    speeds = momenta
    small_q = state[:, 0:2]
    small_p = state[:, 2:4]
    forces, pushes = evaluate(coords, occupied, small_q)
    for step_index in range(STEPS):
        midway_p = speeds + 0.5 * DT * forces
        midway_dp = small_p + 0.5 * DT * pushes
        coords = coords + DT * midway_p
        small_q = small_q + DT * midway_dp
        forces, pushes = evaluate(coords, occupied, small_q)
        speeds = midway_p + 0.5 * DT * forces
        small_p = midway_dp + 0.5 * DT * pushes
    phase = jnp.concatenate([coords, speeds], axis=1)
    final = jnp.concatenate([small_q, small_p], axis=1)
    rows_form = lax.all_to_all(final, "tangent", split_axis=2, concat_axis=3, tiled=True)
    full_width = rows_form.shape[3]
    flat_rows = rows_form.reshape(-1, full_width)
    partial_value = lax.dot_general(
        flat_rows,
        flat_rows,
        (((0,), (0,)), ((), ())),
        precision=HIGH,
        preferred_element_type=jnp.float32,
    )
    gram_scale = 1.0 / (4.0 * slot_count * cell_total * lax.axis_size("space"))
    gram = lax.psum(partial_value, ("space", "tangent"))
    factor = jnp.linalg.cholesky(gram * gram_scale)
    solved = jax.scipy.linalg.solve_triangular(factor, flat_rows.T, lower=True).T
    columns_out = lax.all_to_all(
        solved.reshape(rows_form.shape), "tangent", split_axis=3, concat_axis=2, tiled=True
    )
    log_diag = jnp.log(jnp.diagonal(factor))
    stretch = lax.dynamic_slice_in_dim(log_diag, lax.axis_index("tangent") * block_cols, block_cols)
    return (phase, columns_out, stretch)


def solution(mesh):
    placed = (
        P(("groups", "space"), None, None),
        P(("groups", "space"), None, None),
        P(("groups", "space")),
        P(("groups", "space"), None, None, "tangent"),
    )
    return jax.shard_map(
        body,
        mesh=mesh,
        in_specs=placed,
        out_specs=(
            P(("groups", "space"), None, None),
            P(("groups", "space"), None, None, "tangent"),
            P(("groups", "tangent")),
        ),
        check_vma=False,
    )
```

profile of v0, /device:TPU:1, one launch (start us, length us, event | category | flops | bytes accessed | tf_op | source)
XLA Modules:
  0.0 639.7 jit_solution(17771305510368086692)
XLA Ops:
  8.1 4.2 collective-permute-start.1
  59.8 4.8 collective-permute-done.9
  86.5 7.0 %collective-permute-done.10 = bf16[2,2,128,256]{3,2,0,1:T(8,128)(2,1)S(1)} collective-permute-done((bf16[2,2,128,256]{3,2,0,1:T(8,128)(2,1)S(1)}, bf16[2,2,128,256]{3,2,0,1:T(8,128)(2,1)S(1)}, u32[]{:S(2)}, u32[]{:S(2)}) %collective-permute-start.10) | collective-permute-done | bytes 262176 | tf_op jit(solution)/shard_map/ppermute | solution.py:19
  105.5 21.8 %all_to_all.33 = f32[2,4,128,256]{3,0,1,2:T(2,128)S(1)} all-to-all(f32[2,4,128,256]{3,0,1,2:T(2,128)S(1)} %copy.18), channel_id=1, replica_groups=mesh['groups'=2,'space'=4,'tangent'=4] {'tangent'}, dimensions={2} | all-to-all | bytes 2097152 | tf_op jit(solution)/shard_map/all_to_all | solution.py:146
  128.2 5.2 fusion.2420
  133.8 107.8 %all-reduce.3.cloned.1.call-done = f32[1024,1024]{0,1:T(8,128)} async-done(((f32[1024,1024]{0,1:T(8,128)}), f32[1024,1024]{0,1:T(8,128)}) %all-reduce.3.cloned.1.call-update) | async-done | bytes 4194320 | tf_op jit(solution)/shard_map/psum | solution.py:157
  241.6 5.0 broadcast_multiply_fusion
  246.6 5.7 copy.21
  252.3 4.4 fusion
  258.7 11.7 %cholesky.187 = f32[128,128]{1,0:T(8,128)S(1)} custom-call(f32[128,128]{1,0:T(8,128)S(1)} %cholesky.514), custom_call_target="Cholesky" | custom-call | tf_op jit(solution)/shard_map/jit(cholesky)/cholesky | solution.py:158
  271.1 9.8 %custom-call.63 = f32[1,128,128]{1,2,0:T(8,128)S(1)} custom-call(f32[1,128,128]{2,1,0:T(8,128)S(1)} %get-tuple-element.432), custom_call_target="InvertDiagBlocksLowerTriangular" | custom-call | tf_op jit(solution)/shard_map/jit(cholesky)/cholesky | solution.py:158
  287.3 11.9 %cholesky.209 = f32[128,128]{1,0:T(8,128)S(1)} custom-call(f32[128,128]{1,0:T(8,128)S(1)} %cholesky.518), custom_call_target="Cholesky" | custom-call | tf_op jit(solution)/shard_map/jit(cholesky)/cholesky | solution.py:158
  300.5 9.8 %custom-call.64 = f32[1,128,128]{1,2,0:T(8,128)S(1)} custom-call(f32[1,128,128]{2,1,0:T(8,128)S(1)} %get-tuple-element.429), custom_call_target="InvertDiagBlocksLowerTriangular" | custom-call | tf_op jit(solution)/shard_map/jit(cholesky)/cholesky | solution.py:158
  313.6 11.7 %cholesky.402 = f32[128,128]{1,0:T(8,128)S(1)} custom-call(f32[128,128]{1,0:T(8,128)S(1)} %cholesky.523), custom_call_target="Cholesky" | custom-call | tf_op jit(solution)/shard_map/jit(cholesky)/cholesky | solution.py:158
  326.6 9.8 %custom-call.65 = f32[1,128,128]{1,2,0:T(8,128)S(1)} custom-call(f32[1,128,128]{2,1,0:T(8,128)S(1)} %get-tuple-element.426), custom_call_target="InvertDiagBlocksLowerTriangular" | custom-call | tf_op jit(solution)/shard_map/jit(cholesky)/cholesky | solution.py:158
  340.0 11.9 %cholesky.421 = f32[128,128]{1,0:T(8,128)S(1)} custom-call(f32[128,128]{1,0:T(8,128)S(1)} %cholesky.528), custom_call_target="Cholesky" | custom-call | tf_op jit(solution)/shard_map/jit(cholesky)/cholesky | solution.py:158
  353.3 9.8 %custom-call.66 = f32[1,128,128]{1,2,0:T(8,128)S(1)} custom-call(f32[1,128,128]{2,1,0:T(8,128)S(1)} %get-tuple-element.423), custom_call_target="InvertDiagBlocksLowerTriangular" | custom-call | tf_op jit(solution)/shard_map/jit(cholesky)/cholesky | solution.py:158
  366.5 11.7 %cholesky.440 = f32[128,128]{1,0:T(8,128)S(1)} custom-call(f32[128,128]{1,0:T(8,128)S(1)} %cholesky.533), custom_call_target="Cholesky" | custom-call | tf_op jit(solution)/shard_map/jit(cholesky)/cholesky | solution.py:158
  379.6 10.2 %custom-call.67 = f32[1,128,128]{1,2,0:T(8,128)S(1)} custom-call(f32[1,128,128]{2,1,0:T(8,128)S(1)} %get-tuple-element.420), custom_call_target="InvertDiagBlocksLowerTriangular" | custom-call | tf_op jit(solution)/shard_map/jit(cholesky)/cholesky | solution.py:158
  393.1 11.7 %cholesky.460 = f32[128,128]{1,0:T(8,128)S(1)} custom-call(f32[128,128]{1,0:T(8,128)S(1)} %cholesky.538), custom_call_target="Cholesky" | custom-call | tf_op jit(solution)/shard_map/jit(cholesky)/cholesky | solution.py:158
  406.1 9.8 %custom-call.68 = f32[1,128,128]{1,2,0:T(8,128)S(1)} custom-call(f32[1,128,128]{2,1,0:T(8,128)S(1)} %get-tuple-element.417), custom_call_target="InvertDiagBlocksLowerTriangular" | custom-call | tf_op jit(solution)/shard_map/jit(cholesky)/cholesky | solution.py:158
  418.9 11.9 %cholesky.480 = f32[128,128]{1,0:T(8,128)S(1)} custom-call(f32[128,128]{1,0:T(8,128)S(1)} %cholesky.543), custom_call_target="Cholesky" | custom-call | tf_op jit(solution)/shard_map/jit(cholesky)/cholesky | solution.py:158
  432.1 9.8 %custom-call.69 = f32[1,128,128]{1,2,0:T(8,128)S(1)} custom-call(f32[1,128,128]{2,1,0:T(8,128)S(1)} %get-tuple-element.414), custom_call_target="InvertDiagBlocksLowerTriangular" | custom-call | tf_op jit(solution)/shard_map/jit(cholesky)/cholesky | solution.py:158
  444.5 11.7 %cholesky.498 = f32[128,128]{1,0:T(8,128)S(1)} custom-call(f32[128,128]{1,0:T(8,128)S(1)} %convolution_subtract_fusion.13), custom_call_target="Cholesky" | custom-call | tf_op jit(solution)/shard_map/jit(cholesky)/cholesky | solution.py:158
  462.6 6.6 %fusion.1 = (f32[1024,1024]{1,0:T(8,128)}, f32[1024,1024]{1,0:T(8,128)}) fusion(f32[1024,1024]{1,0:T(8,128)} %get-tuple-element.412, pred[]{:T(512)S(6)} %cholesky.513), kind=kLoop, calls=%fused_computation.7 | loop fusion | flops 4194304 | bytes 12582913 | tf_op jit(solution)/shard_map/jit(_solve_triangular)/triangular_solve | solution.py:159
  469.2 23.2 %while.1 = (s32[]{:T(128)}, f32[1024,1024]{1,0:T(8,128)}, s32[8,2]{0,1:T(2,128)S(1)}, f32[8,128,128]{2,1,0:T(8,128)S(1)}, s32[]{:T(128)}) while((s32[]{:T(128)}, f32[1024,1024]{1,0:T(8,128)}, s32[8,2]{0,1:T(2,128)S(1)}, f32[8,128,128]{2,1,0:T(8,128)S(1)}, s32[]{:T(128)}) %tuple.396), condition=%wide.while_cond, body=%wide.while_body.sunk | while | flops 2 | bytes 131189 | solution.py:159
  492.4 79.4 %custom-call.70 = f32[8,128,128]{1,2,0:T(8,128)} custom-call(f32[8,128,128]{2,1,0:T(8,128)S(1)} %get-tuple-element.10), custom_call_target="InvertDiagBlocksLowerTriangular" | custom-call | tf_op jit(solution)/shard_map/jit(_solve_triangular)/triangular_solve | solution.py:159
  590.1 5.3 reshape.847
  595.5 5.5 all-to-all-start.1
  601.7 17.3 %gather_fusion = f32[1024]{0:T(1024)S(1)} fusion(f32[1024,1024]{1,0:T(8,128)} %get-tuple-element.320, s32[1024]{0:T(1024)S(1)} %bitcast.397), kind=kCustom, calls=%fused_computation | custom fusion | bytes 16384 | tf_op jit(solution)/shard_map/jit(diagonal)/cond/branch_0_fun/gather | solution.py:163
  623.8 4.2 reshape.848
  628.1 4.6 copy.25
  (318 shorter events, 167.2 us)
Async XLA Ops:
  7.2 234.4 %all-reduce.3.cloned.1.call-start = ((), (), s32[]{:S(2)}) async-start(), calls=%async_computation.2 | async-start | bytes 8388608 | tf_op jit(solution)/shard_map/psum | solution.py:157
  8.1 12.2 %collective-permute-start.1 = (f32[2,2,128]{2,1,0:T(2,128)S(1)}, f32[2,2,128]{2,1,0:T(2,128)S(1)}, u32[]{:S(2)}, u32[]{:S(2)}) collective-permute-start(f32[2,2,128]{2,1,0:T(2,128)S(1)} %pad_maximum_fusion.11), channel_id=1, source_target_pairs={{4,0},{8,4},{12,8},{0,12},{5,1},{9,5},{13,9},{1,13},{6,2},{10,6},{... | collective-permute-start | bytes 6152 | tf_op jit(solution)/shard_map/ppermute | solution.py:22
  12.3 8.1 %collective-permute-start = (f32[2,2,128]{2,1,0:T(2,128)S(1)}, f32[2,2,128]{2,1,0:T(2,128)S(1)}, u32[]{:S(2)}, u32[]{:S(2)}) collective-permute-start(f32[2,2,128]{2,1,0:T(2,128)S(1)} %pad_maximum_fusion.11), channel_id=1, source_target_pairs={{0,4},{4,8},{8,12},{12,0},{1,5},{5,9},{9,13},{13,1},{2,6},{6,10},{... | collective-permute-start | bytes 6152 | tf_op jit(solution)/shard_map/ppermute | solution.py:19
  14.4 28.2 %collective-permute-start.7 = (bf16[2,2,128,256]{3,2,0,1:T(8,128)(2,1)S(1)}, bf16[2,2,128,256]{3,2,0,1:T(8,128)(2,1)S(1)}, u32[]{:S(2)}, u32[]{:S(2)}) collective-permute-start(bf16[2,2,128,256]{3,2,0,1:T(8,128)(2,1)S(1)} %get-tuple-element.327), channel_id=1, source_target_pairs={{4,0},{8,4},{12,8},{0,12},{5,1},{9,5},{13,9},{1,13},{6,2},{10,6},{... | collective-permute-start | bytes 786440 | tf_op jit(solution)/shard_map/ppermute | solution.py:22
  17.7 26.6 %collective-permute-start.6 = (bf16[2,2,128,256]{3,2,0,1:T(8,128)(2,1)S(1)}, bf16[2,2,128,256]{3,2,0,1:T(8,128)(2,1)S(1)}, u32[]{:S(2)}, u32[]{:S(2)}) collective-permute-start(bf16[2,2,128,256]{3,2,0,1:T(8,128)(2,1)S(1)} %get-tuple-element.327), channel_id=1, source_target_pairs={{0,4},{4,8},{8,12},{12,0},{1,5},{5,9},{9,13},{13,1},{2,6},{6,10},{... | collective-permute-start | bytes 786440 | tf_op jit(solution)/shard_map/ppermute | solution.py:19
  18.6 4.9 copy-start.3
  18.6 4.9 copy-start.4
  18.7 4.9 copy-start.2
  23.7 4.2 collective-permute-start.3
  27.0 4.2 collective-permute-start.2
  34.6 2.5 collective-permute-start.5
  35.0 4.2 collective-permute-start.4
  57.1 7.5 %collective-permute-start.9 = (bf16[2,2,128,256]{3,2,0,1:T(8,128)(2,1)S(1)}, bf16[2,2,128,256]{3,2,0,1:T(8,128)(2,1)S(1)}, u32[]{:S(2)}, u32[]{:S(2)}) collective-permute-start(bf16[2,2,128,256]{3,2,0,1:T(8,128)(2,1)S(1)} %get-tuple-element.325), channel_id=1, source_target_pairs={{4,0},{8,4},{12,8},{0,12},{5,1},{9,5},{13,9},{1,13},{6,2},{10,6},{... | collective-permute-start | bytes 786440 | tf_op jit(solution)/shard_map/ppermute | solution.py:22
  58.0 8.5 %collective-permute-start.8 = (bf16[2,2,128,256]{3,2,0,1:T(8,128)(2,1)S(1)}, bf16[2,2,128,256]{3,2,0,1:T(8,128)(2,1)S(1)}, u32[]{:S(2)}, u32[]{:S(2)}) collective-permute-start(bf16[2,2,128,256]{3,2,0,1:T(8,128)(2,1)S(1)} %get-tuple-element.325), channel_id=1, source_target_pairs={{0,4},{4,8},{8,12},{12,0},{1,5},{5,9},{9,13},{13,1},{2,6},{6,10},{... | collective-permute-start | bytes 786440 | tf_op jit(solution)/shard_map/ppermute | solution.py:19
  79.4 5.5 collective-permute-start.11
  80.8 12.8 %collective-permute-start.10 = (bf16[2,2,128,256]{3,2,0,1:T(8,128)(2,1)S(1)}, bf16[2,2,128,256]{3,2,0,1:T(8,128)(2,1)S(1)}, u32[]{:S(2)}, u32[]{:S(2)}) collective-permute-start(bf16[2,2,128,256]{3,2,0,1:T(8,128)(2,1)S(1)} %get-tuple-element.322), channel_id=1, source_target_pairs={{0,4},{4,8},{8,12},{12,0},{1,5},{5,9},{9,13},{13,1},{2,6},{6,10},{... | collective-permute-start | bytes 786440 | tf_op jit(solution)/shard_map/ppermute | solution.py:19
  256.8 1.9 copy-start
  571.8 7.2 %copy-start.1 = (f32[8,128,128]{1,2,0:T(8,128)S(1)}, f32[8,128,128]{1,2,0:T(8,128)}, u32[]{:S(2)}) copy-start(f32[8,128,128]{1,2,0:T(8,128)} %custom-call.70) | copy-start | bytes 1572868
  595.5 24.2 %all-to-all-start.1 = ((f32[4,1,65536]{2,1,0:T(1,128)}), f32[4,1,65536]{2,1,0:T(1,128)S(1)}, u32[]{:S(2)}, u32[]{:S(2)}) async-start(f32[4,1,65536]{2,1,0:T(1,128)} %reshape.847), calls=%async_computation.1 | async-start | bytes 2097152 | tf_op jit(solution)/shard_map/all_to_all | solution.py:160
Sparse Core Ops, SparseCore 0:
  133.6 107.9 all-reduce.2
where the time goes:
time: 647 us; the launch traced here: 640 us
  other arithmetic  287 us (44%)
  waiting for transfers between devices  130 us (20%)
  matrix products  87.6 us (14%)
  local copies, waits for them, and re-layouts  71.5 us (11%)
  starting transfers between devices  21.9 us (3%)
  blocking collectives  21.8 us (3%)
  between operations  20.3 us (3%)
    another operation x31, other arithmetic, body(): factor = jnp.linalg.cholesky(gram * gram_scale)  173 us
    psum x1, waiting for transfers between devices, body(): gram = lax.psum(partial_value, ('space', 'tangent'))  108 us
    another operation x3, other arithmetic, body(): jax.scipy.linalg.solve_triangular(factor, flat_rows.T, lower=True)  86 us
    another operation x14, matrix products, body(): factor = jnp.linalg.cholesky(gram * gram_scale)  23.1 us
    another operation x24, local copies, waits for them, and re-layouts  23 us
    all_to_all x1, blocking collectives, body(): lax.all_to_all(final, 'tangent', split_axis=2, concat_axis=3, tiled=True)  21.8 us
    gather x1, local copies, waits for them, and re-layouts, body(): log_diag = jnp.log(jnp.diagonal(factor))  17.3 us
    another operation x15, matrix products, body(): jax.scipy.linalg.solve_triangular(factor, flat_rows.T, lower=True)  14.7 us
  transfers between devices with their start and end apart: 14, of which 9 were waited for; matrix products, arithmetic and copies ran while one was open for 6% of the time, Pallas kernels for 0%

commit v1 on v0

--- a/solution.py
+++ b/solution.py
@@ -154,7 +154,7 @@
         preferred_element_type=jnp.float32,
     )
     gram_scale = 1.0 / (4.0 * slot_count * cell_total * lax.axis_size("space"))
-    gram = lax.psum(partial_value, ("space", "tangent"))
+    gram = jnp.sum(lax.all_gather(partial_value, ("space", "tangent")), axis=0)
     factor = jnp.linalg.cholesky(gram * gram_scale)
     solved = jax.scipy.linalg.solve_triangular(factor, flat_rows.T, lower=True).T
     columns_out = lax.all_to_all(

time: 647 us -> 874 us (1.35)
  waiting for transfers between devices: 130 us -> 341 us
  other arithmetic: 287 us -> 304 us
    all_gather x0 -> x1, waiting for transfers between devices: none -> 325 us  [body(): gram = jnp.sum(lax.all_gather(partial_value, ('space', 'tangent')), axis=0)]
    psum x1 -> x0, waiting for transfers between devices: 108 us -> none  [body(): gram = lax.psum(partial_value, ('space', 'tangent'))]
    reduce_sum x0 -> x1, other arithmetic: none -> 22.9 us  [body(): gram = jnp.sum(lax.all_gather(partial_value, ('space', 'tangent')), axis=0)]
  transfers between devices with their start and end apart: 14 -> 14, of which waited for: 9 -> 7; matrix products, arithmetic and copies ran while one was open for 6% -> 5% of each run, Pallas kernels for 0% -> 0%
where the time goes in v1:
time: 874 us; the launch traced here: 867 us
  waiting for transfers between devices  341 us (39%)
  other arithmetic  304 us (35%)
  matrix products  87.6 us (10%)
  local copies, waits for them, and re-layouts  71.5 us (8%)
  starting transfers between devices  22.2 us (3%)
  between operations  20.4 us (2%)
  blocking collectives  19.7 us (2%)
    all_gather x1, waiting for transfers between devices, body(): gram = jnp.sum(lax.all_gather(partial_value, ('space', 'tangent')), axis=0)  325 us
    another operation x31, other arithmetic, body(): factor = jnp.linalg.cholesky(gram * gram_scale)  173 us
    another operation x3, other arithmetic, body(): jax.scipy.linalg.solve_triangular(factor, flat_rows.T, lower=True)  86 us
    another operation x14, matrix products, body(): factor = jnp.linalg.cholesky(gram * gram_scale)  23.1 us
    another operation x24, local copies, waits for them, and re-layouts  23 us
    reduce_sum x1, other arithmetic, body(): gram = jnp.sum(lax.all_gather(partial_value, ('space', 'tangent')), axis=0)  22.9 us
    all_to_all x1, blocking collectives, body(): lax.all_to_all(final, 'tangent', split_axis=2, concat_axis=3, tiled=True)  19.7 us
  transfers between devices with their start and end apart: 14, of which 7 were waited for; matrix products, arithmetic and copies ran while one was open for 5% of the time, Pallas kernels for 0%

profile of v1, /device:TPU:1, one launch (start us, length us, event | category | flops | bytes accessed | tf_op | source)
XLA Modules:
  0.0 866.9 jit_solution(14498308853528486400)
XLA Ops:
  56.9 7.1 collective-permute-done.8
  81.0 7.2 collective-permute-done.10
  101.9 19.7 %all_to_all.33 = f32[2,4,128,256]{3,0,1,2:T(2,128)S(1)} all-to-all(f32[2,4,128,256]{3,0,1,2:T(2,128)S(1)} %copy.16), channel_id=1, replica_groups=mesh['groups'=2,'space'=4,'tangent'=4] {'tangent'}, dimensions={2} | all-to-all | bytes 2097152 | tf_op jit(solution)/shard_map/all_to_all | solution.py:146
  122.4 5.1 fusion.2420
  128.0 324.6 %all-gather.3.cloned.1.call-done = f32[16384,1024]{1,0:T(8,128)} async-done(((f32[1024,1024]{1,0:T(8,128)}), f32[16384,1024]{1,0:T(8,128)}) %all-gather.3.cloned.1.call-update) | async-done | bytes 67108880 | tf_op jit(solution)/shard_map/all_gather | solution.py:157
  452.6 22.9 %reduce_sum.1433 = f32[1024,1024]{1,0:T(8,128)} reduce(f32[16,1024,1024]{2,1,0:T(8,128)} %bitcast.101, f32[]{:T(128)} %constant.447.clone.1), dimensions={0}, to_apply=%region_135.136 | reduce | flops 15728640 | bytes 71303168 | tf_op jit(solution)/shard_map/reduce_sum | solution.py:157
  475.5 5.7 copy.18
  481.2 4.4 fusion
  487.6 11.7 %cholesky.187 = f32[128,128]{1,0:T(8,128)S(1)} custom-call(f32[128,128]{1,0:T(8,128)S(1)} %cholesky.514), custom_call_target="Cholesky" | custom-call | tf_op jit(solution)/shard_map/jit(cholesky)/cholesky | solution.py:158
  501.9 9.8 %custom-call.63 = f32[1,128,128]{1,2,0:T(8,128)S(1)} custom-call(f32[1,128,128]{2,1,0:T(8,128)S(1)} %get-tuple-element.432), custom_call_target="InvertDiagBlocksLowerTriangular" | custom-call | tf_op jit(solution)/shard_map/jit(cholesky)/cholesky | solution.py:158
  515.6 11.9 %cholesky.209 = f32[128,128]{1,0:T(8,128)S(1)} custom-call(f32[128,128]{1,0:T(8,128)S(1)} %cholesky.518), custom_call_target="Cholesky" | custom-call | tf_op jit(solution)/shard_map/jit(cholesky)/cholesky | solution.py:158
  528.1 9.8 %custom-call.64 = f32[1,128,128]{1,2,0:T(8,128)S(1)} custom-call(f32[1,128,128]{2,1,0:T(8,128)S(1)} %get-tuple-element.429), custom_call_target="InvertDiagBlocksLowerTriangular" | custom-call | tf_op jit(solution)/shard_map/jit(cholesky)/cholesky | solution.py:158
  541.3 11.7 %cholesky.402 = f32[128,128]{1,0:T(8,128)S(1)} custom-call(f32[128,128]{1,0:T(8,128)S(1)} %cholesky.523), custom_call_target="Cholesky" | custom-call | tf_op jit(solution)/shard_map/jit(cholesky)/cholesky | solution.py:158
  553.6 9.8 %custom-call.65 = f32[1,128,128]{1,2,0:T(8,128)S(1)} custom-call(f32[1,128,128]{2,1,0:T(8,128)S(1)} %get-tuple-element.426), custom_call_target="InvertDiagBlocksLowerTriangular" | custom-call | tf_op jit(solution)/shard_map/jit(cholesky)/cholesky | solution.py:158
  567.0 11.9 %cholesky.421 = f32[128,128]{1,0:T(8,128)S(1)} custom-call(f32[128,128]{1,0:T(8,128)S(1)} %cholesky.528), custom_call_target="Cholesky" | custom-call | tf_op jit(solution)/shard_map/jit(cholesky)/cholesky | solution.py:158
  579.6 9.8 %custom-call.66 = f32[1,128,128]{1,2,0:T(8,128)S(1)} custom-call(f32[1,128,128]{2,1,0:T(8,128)S(1)} %get-tuple-element.423), custom_call_target="InvertDiagBlocksLowerTriangular" | custom-call | tf_op jit(solution)/shard_map/jit(cholesky)/cholesky | solution.py:158
  592.8 11.7 %cholesky.440 = f32[128,128]{1,0:T(8,128)S(1)} custom-call(f32[128,128]{1,0:T(8,128)S(1)} %cholesky.533), custom_call_target="Cholesky" | custom-call | tf_op jit(solution)/shard_map/jit(cholesky)/cholesky | solution.py:158
  605.2 10.2 %custom-call.67 = f32[1,128,128]{1,2,0:T(8,128)S(1)} custom-call(f32[1,128,128]{2,1,0:T(8,128)S(1)} %get-tuple-element.420), custom_call_target="InvertDiagBlocksLowerTriangular" | custom-call | tf_op jit(solution)/shard_map/jit(cholesky)/cholesky | solution.py:158
  618.7 11.7 %cholesky.460 = f32[128,128]{1,0:T(8,128)S(1)} custom-call(f32[128,128]{1,0:T(8,128)S(1)} %cholesky.538), custom_call_target="Cholesky" | custom-call | tf_op jit(solution)/shard_map/jit(cholesky)/cholesky | solution.py:158
  631.1 9.8 %custom-call.68 = f32[1,128,128]{1,2,0:T(8,128)S(1)} custom-call(f32[1,128,128]{2,1,0:T(8,128)S(1)} %get-tuple-element.417), custom_call_target="InvertDiagBlocksLowerTriangular" | custom-call | tf_op jit(solution)/shard_map/jit(cholesky)/cholesky | solution.py:158
  643.9 11.7 %cholesky.480 = f32[128,128]{1,0:T(8,128)S(1)} custom-call(f32[128,128]{1,0:T(8,128)S(1)} %cholesky.543), custom_call_target="Cholesky" | custom-call | tf_op jit(solution)/shard_map/jit(cholesky)/cholesky | solution.py:158
  656.3 9.8 %custom-call.69 = f32[1,128,128]{1,2,0:T(8,128)S(1)} custom-call(f32[1,128,128]{2,1,0:T(8,128)S(1)} %get-tuple-element.414), custom_call_target="InvertDiagBlocksLowerTriangular" | custom-call | tf_op jit(solution)/shard_map/jit(cholesky)/cholesky | solution.py:158
  668.7 11.7 %cholesky.498 = f32[128,128]{1,0:T(8,128)S(1)} custom-call(f32[128,128]{1,0:T(8,128)S(1)} %convolution_subtract_fusion.13), custom_call_target="Cholesky" | custom-call | tf_op jit(solution)/shard_map/jit(cholesky)/cholesky | solution.py:158
  691.4 6.6 fusion.1
  698.0 23.2 %while.1 = (s32[]{:T(128)}, f32[1024,1024]{1,0:T(8,128)}, s32[8,2]{0,1:T(2,128)S(1)}, f32[8,128,128]{2,1,0:T(8,128)S(1)}, s32[]{:T(128)}) while((s32[]{:T(128)}, f32[1024,1024]{1,0:T(8,128)}, s32[8,2]{0,1:T(2,128)S(1)}, f32[8,128,128]{2,1,0:T(8,128)S(1)}, s32[]{:T(128)}) %tuple.396), condition=%wide.while_cond, body=%wide.while_body.sunk | while | flops 2 | bytes 131189 | solution.py:159
  721.2 79.4 %custom-call.70 = f32[8,128,128]{1,2,0:T(8,128)} custom-call(f32[8,128,128]{2,1,0:T(8,128)S(1)} %get-tuple-element.10), custom_call_target="InvertDiagBlocksLowerTriangular" | custom-call | tf_op jit(solution)/shard_map/jit(_solve_triangular)/triangular_solve | solution.py:159
  818.9 5.3 reshape.848
  824.3 4.0 all-to-all-start.1
  828.9 17.3 %gather_fusion = f32[1024]{0:T(1024)S(1)} fusion(f32[1024,1024]{1,0:T(8,128)} %get-tuple-element.320, s32[1024]{0:T(1024)S(1)} %bitcast.398), kind=kCustom, calls=%fused_computation | custom fusion | bytes 16384 | tf_op jit(solution)/shard_map/jit(diagonal)/cond/branch_0_fun/gather | solution.py:163
  847.4 3.7 reduce.48
  851.1 4.2 reshape.849
  855.3 4.6 copy.22
  (318 shorter events, 161.5 us)
Async XLA Ops:
  7.2 445.4 %all-gather.3.cloned.1.call-start = ((), (), s32[]{:S(2)}) async-start(), calls=%async_computation.2 | async-start | bytes 71303168 | tf_op jit(solution)/shard_map/all_gather | solution.py:157
  8.1 10.5 %collective-permute-start = (f32[2,2,128]{2,1,0:T(2,128)S(1)}, f32[2,2,128]{2,1,0:T(2,128)S(1)}, u32[]{:S(2)}, u32[]{:S(2)}) collective-permute-start(f32[2,2,128]{2,1,0:T(2,128)S(1)} %pad_maximum_fusion.11), channel_id=1, source_target_pairs={{0,4},{4,8},{8,12},{12,0},{1,5},{5,9},{9,13},{13,1},{2,6},{6,10},{... | collective-permute-start | bytes 6152 | tf_op jit(solution)/shard_map/ppermute | solution.py:19
  10.2 8.3 collective-permute-start.1
  14.5 24.1 %collective-permute-start.7 = (bf16[2,2,128,256]{3,2,0,1:T(8,128)(2,1)S(1)}, bf16[2,2,128,256]{3,2,0,1:T(8,128)(2,1)S(1)}, u32[]{:S(2)}, u32[]{:S(2)}) collective-permute-start(bf16[2,2,128,256]{3,2,0,1:T(8,128)(2,1)S(1)} %get-tuple-element.327), channel_id=1, source_target_pairs={{4,0},{8,4},{12,8},{0,12},{5,1},{9,5},{13,9},{1,13},{6,2},{10,6},{... | collective-permute-start | bytes 786440 | tf_op jit(solution)/shard_map/ppermute | solution.py:22
  15.9 21.8 %collective-permute-start.6 = (bf16[2,2,128,256]{3,2,0,1:T(8,128)(2,1)S(1)}, bf16[2,2,128,256]{3,2,0,1:T(8,128)(2,1)S(1)}, u32[]{:S(2)}, u32[]{:S(2)}) collective-permute-start(bf16[2,2,128,256]{3,2,0,1:T(8,128)(2,1)S(1)} %get-tuple-element.327), channel_id=1, source_target_pairs={{0,4},{4,8},{8,12},{12,0},{1,5},{5,9},{9,13},{13,1},{2,6},{6,10},{... | collective-permute-start | bytes 786440 | tf_op jit(solution)/shard_map/ppermute | solution.py:19
  16.9 4.9 copy-start.3
  16.9 4.9 copy-start.4
  16.9 4.9 copy-start.2
  21.9 4.9 collective-permute-start.2
  22.0 4.1 collective-permute-start.3
  30.2 4.3 collective-permute-start.4
  31.6 2.8 collective-permute-start.5
  50.5 14.3 %collective-permute-start.9 = (bf16[2,2,128,256]{3,2,0,1:T(8,128)(2,1)S(1)}, bf16[2,2,128,256]{3,2,0,1:T(8,128)(2,1)S(1)}, u32[]{:S(2)}, u32[]{:S(2)}) collective-permute-start(bf16[2,2,128,256]{3,2,0,1:T(8,128)(2,1)S(1)} %get-tuple-element.325), channel_id=1, source_target_pairs={{4,0},{8,4},{12,8},{0,12},{5,1},{9,5},{13,9},{1,13},{6,2},{10,6},{... | collective-permute-start | bytes 786440 | tf_op jit(solution)/shard_map/ppermute | solution.py:22
  54.0 10.0 %collective-permute-start.8 = (bf16[2,2,128,256]{3,2,0,1:T(8,128)(2,1)S(1)}, bf16[2,2,128,256]{3,2,0,1:T(8,128)(2,1)S(1)}, u32[]{:S(2)}, u32[]{:S(2)}) collective-permute-start(bf16[2,2,128,256]{3,2,0,1:T(8,128)(2,1)S(1)} %get-tuple-element.325), channel_id=1, source_target_pairs={{0,4},{4,8},{8,12},{12,0},{1,5},{5,9},{9,13},{13,1},{2,6},{6,10},{... | collective-permute-start | bytes 786440 | tf_op jit(solution)/shard_map/ppermute | solution.py:19
  76.8 12.2 %collective-permute-start.11 = (bf16[2,2,128,256]{3,2,0,1:T(8,128)(2,1)S(1)}, bf16[2,2,128,256]{3,2,0,1:T(8,128)(2,1)S(1)}, u32[]{:S(2)}, u32[]{:S(2)}) collective-permute-start(bf16[2,2,128,256]{3,2,0,1:T(8,128)(2,1)S(1)} %get-tuple-element.322), channel_id=1, source_target_pairs={{4,0},{8,4},{12,8},{0,12},{5,1},{9,5},{13,9},{1,13},{6,2},{10,6},{... | collective-permute-start | bytes 786440 | tf_op jit(solution)/shard_map/ppermute | solution.py:22
  78.3 9.9 %collective-permute-start.10 = (bf16[2,2,128,256]{3,2,0,1:T(8,128)(2,1)S(1)}, bf16[2,2,128,256]{3,2,0,1:T(8,128)(2,1)S(1)}, u32[]{:S(2)}, u32[]{:S(2)}) collective-permute-start(bf16[2,2,128,256]{3,2,0,1:T(8,128)(2,1)S(1)} %get-tuple-element.322), channel_id=1, source_target_pairs={{0,4},{4,8},{8,12},{12,0},{1,5},{5,9},{9,13},{13,1},{2,6},{6,10},{... | collective-permute-start | bytes 786440 | tf_op jit(solution)/shard_map/ppermute | solution.py:19
  485.7 1.9 copy-start
  800.6 7.2 copy-start.1
  824.3 22.6 %all-to-all-start.1 = ((f32[4,1,65536]{2,1,0:T(1,128)}), f32[4,1,65536]{2,1,0:T(1,128)S(1)}, u32[]{:S(2)}, u32[]{:S(2)}) async-start(f32[4,1,65536]{2,1,0:T(1,128)} %reshape.848), calls=%async_computation.1 | async-start | bytes 2097152 | tf_op jit(solution)/shard_map/all_to_all | solution.py:160
Sparse Core Ops, SparseCore 0:
  127.7 324.8 all-gather.2
